TPU v7x, 32 devices: a whole 2x2x4 slice. The times are simulated.
32 devices in a mesh: grp: 4 (over x, core), sub: 8 (over z, y).
Axes of the slice: x: 2, y: 2, z: 4, core: 2. Of those that a mesh axis runs over, the one named last changes fastest.
Arguments:
- right_side: float32 [65536, 128], P(('grp', 'sub')), may hold values from -6 to 6
- fine_values: float32 [81, 65536], P(None, ('grp', 'sub')), as said below
- columns: int32 [81, 65536], P(None, ('grp', 'sub')), may hold values from 0 to 2175, as said below
- agg_map: int32 [65536], P(('grp', 'sub')), may hold values from 0 to 127
- send_lo: int32 [2048], P(('grp', 'sub')), may hold values from 0 to 2047
- send_hi: int32 [2048], P(('grp', 'sub')), may hold values from 0 to 2047
- coarse_matrix: float32 [4, 1024, 1024], P('grp', 'sub'), as said below
Outputs:
- solution: float32 [65536, 128], P(('grp', 'sub'))
- residual: float32 [65536, 128], P(('grp', 'sub'))
Inputs may be any that keep to these rules, and one draw needn't show every extreme that they name: `columns`: entry 0 of row i of a partition is 64 + i, the others lie within 64 positions of it. `fine_values`: entry 0 lies in 2.5 to 5 and every other entry's magnitude is at most 0.06. `coarse_matrix`: symmetric; the diagonal lies in 10 to 20, other entries' magnitudes are at most 7.1 / sqrt(1024).
All inputs are finite; a program needn't handle non-finite values.
Results may differ from a plain program's by a relative error of at most 0.0001.
Values sent between devices are 32-bit elements; how exact they have to be, the bound alone decides.
A program may use at most 128 MiB of HBM per device.

v0:
```python
import jax
import jax.numpy as jnp
from jax import lax
from jax.sharding import PartitionSpec as P

CHEB_FINE = 2
CHEB_COARSE = 6
CYCLES = 2
THETA = 1.0
DELTA = 0.7
OMEGA = 0.6
highest = lax.Precision.HIGHEST


def from_behind(shard, axis, by):
    peers = lax.axis_size(axis)
    pairs = [(i, i + by) for i in range(peers) if 0 <= i + by < peers]
    return lax.ppermute(shard, axis, pairs)


def band_tiles(fine_values, columns, block_rows):
    rows_dev = columns.shape[1]
    rows = jnp.arange(rows_dev, dtype=jnp.int32)
    starts = rows // block_rows * block_rows
    local = columns - starts[None, :]
    places = jnp.arange(2 * block_rows, dtype=jnp.int32)[None, :]
    tiles = jnp.zeros((rows_dev, 2 * block_rows), jnp.float32)
    for entry in range(columns.shape[0]):
        tiles = tiles + jnp.where(local[entry][:, None] == places, fine_values[entry][:, None], 0.0)
    tiles = tiles.reshape(rows_dev // block_rows, block_rows, 2 * block_rows)
    return (tiles[:, :, :block_rows], tiles[:, :, block_rows:])


def selector(indices, count):
    return (indices[:, None] == jnp.arange(count, dtype=jnp.int32)[None, :]).astype(jnp.float32)


def fine_apply(vector, low_tiles, high_tiles, pick_lo, pick_hi):
    upper_rows = jnp.dot(pick_hi, vector, precision=highest)
    lower_rows = jnp.dot(pick_lo, vector, precision=highest)
    below = from_behind(upper_rows, ("grp", "sub"), 1)
    above = from_behind(lower_rows, ("grp", "sub"), -1)
    extended = jnp.concatenate([below, vector, above], 0)
    block_rows = low_tiles.shape[1]
    pieces = extended.reshape(-1, block_rows, vector.shape[1])
    total = jnp.einsum("brc,bcn->brn", low_tiles, pieces[:-1], precision=highest)
    total = total + jnp.einsum("brc,bcn->brn", high_tiles, pieces[1:], precision=highest)
    return total.reshape(vector.shape)


def chebyshev(residual, apply, inverse, steps, final):
    rho_old = DELTA / THETA
    direction = inverse * residual / THETA
    result = direction
    for turn in range(1, steps):
        residual = residual - apply(direction)
        rho_new = 1.0 / (2.0 * THETA / DELTA - rho_old)
        direction = rho_new * rho_old * direction + 2.0 * rho_new / DELTA * inverse * residual
        result = result + direction
        rho_old = rho_new
    if final:
        residual = residual - apply(direction)
    return (result, residual)


def body(right_side, fine_values, columns, agg_map, send_lo, send_hi, coarse_matrix):
    rows_dev = right_side.shape[0]
    low_tiles, high_tiles = band_tiles(fine_values, columns, 2 * send_lo.shape[0])
    pick_lo = selector(send_lo, rows_dev)
    pick_hi = selector(send_hi, rows_dev)

    def apply_fine(vector):
        return fine_apply(vector, low_tiles, high_tiles, pick_lo, pick_hi)

    own_rows = coarse_matrix[0]
    aggregates = own_rows.shape[0]
    sub_index = lax.axis_index("sub")
    start = sub_index * aggregates
    block = lax.dynamic_slice_in_dim(own_rows, start, aggregates, 1)
    coarse_inverse = 1.0 / jnp.diagonal(block)[:, None]

    def apply_coarse(vector):
        whole = lax.all_gather(vector, "sub", axis=0, tiled=True)
        return jnp.dot(own_rows, whole, precision=highest)

    dinv = 1.0 / fine_values[0][:, None]
    onehot = selector(agg_map, aggregates)
    solution = jnp.zeros_like(right_side)
    residual = right_side
    for cycle in range(CYCLES):
        update, residual = chebyshev(residual, apply_fine, dinv, CHEB_FINE, True)
        solution = solution + update
        smoothed = residual - OMEGA * apply_fine(dinv * residual)
        coarse_rhs = jnp.einsum("ra,rn->an", onehot, smoothed, precision=highest)
        result, unused = chebyshev(coarse_rhs, apply_coarse, coarse_inverse, CHEB_COARSE, False)
        spread = jnp.dot(onehot, result, precision=highest)
        correction = spread - OMEGA * dinv * apply_fine(spread)
        solution = solution + correction
        residual = residual - apply_fine(correction)
        update, residual = chebyshev(residual, apply_fine, dinv, CHEB_FINE, True)
        solution = solution + update
    return (solution, residual)


def solution(mesh):
    placed = (
        P(("grp", "sub"), None),
        P(None, ("grp", "sub")),
        P(None, ("grp", "sub")),
        P(("grp", "sub")),
        P(("grp", "sub")),
        P(("grp", "sub")),
        P("grp", "sub", None),
    )
    return jax.shard_map(
        body,
        mesh=mesh,
        in_specs=placed,
        out_specs=(P(("grp", "sub"), None), P(("grp", "sub"), None)),
        check_vma=False,
    )
```

profile of v0, /device:TPU:29, one launch (start us, length us, event | category | flops | bytes accessed | tf_op | source)
XLA Modules:
  0.0 596.2 jit_solution(620123093191027239)
XLA Ops:
  9.6 7.1 %collective-permute-start = (f32[64,128]{1,0:T(8,128)}, f32[64,128]{1,0:T(8,128)S(1)}, u32[]{:S(2)}, u32[]{:S(2)}) collective-permute-start(f32[64,128]{1,0:T(8,128)} %fusion.65), channel_id=1, source_target_pairs={{0,1},{1,2},{2,3},{3,4},{4,5},{5,6},{6,7},{7,8},{8,9},{9,10},{10,1... | collective-permute-start | bytes 98312 | tf_op jit(solution)/shard_map/ppermute | solution.py:18
  21.6 47.7 %select_add_fusion = f32[16,128,256]{2,1,0:T(8,128)S(1)} fusion(f32[16,128]{1,0:T(8,128)S(1)} %bitcast.486, s32[16,128]{1,0:T(8,128)} %bitcast.608, f32[16,128]{1,0:T(8,128)S(1)} %bitcast.487, s32[16,128]{1,0:T(8,128)} %bitcast.609, f32[16,128]{1,0:T(8,128)S(1)} %bitcast.465, s32[16,128]{1,0:T(8,128)} %bitcast.610, f32[16,128]{1,0:T(8,128)S(1)} %bitcast.466, ...), kind=kLoop, calls=%fused_computation.1 | loop fusion | flops 126877696 | bytes 3424256 | tf_op jit(solution)/shard_map/add | solution.py:29
  82.1 5.4 collective-permute-done.3
  107.1 26.0 %all_gather.30 = f32[1024,128]{1,0:T(8,128)S(1)} all-gather(f32[128,128]{1,0:T(8,128)S(1)} %get-tuple-element.209), channel_id=1, replica_groups=mesh['grp'=4,'sub'=8] {'sub'}, dimensions={0}, use_global_device_ids=true | all-gather | bytes 589824 | tf_op jit(solution)/shard_map/all_gather | solution.py:83
  133.8 25.7 %all_gather.31 = f32[1024,128]{1,0:T(8,128)S(1)} all-gather(f32[128,128]{1,0:T(8,128)S(1)} %get-tuple-element.211), channel_id=1, replica_groups=mesh['grp'=4,'sub'=8] {'sub'}, dimensions={0}, use_global_device_ids=true | all-gather | bytes 589824 | tf_op jit(solution)/shard_map/all_gather | solution.py:83
  160.1 25.7 %all_gather.32 = f32[1024,128]{1,0:T(8,128)S(1)} all-gather(f32[128,128]{1,0:T(8,128)S(1)} %get-tuple-element.213), channel_id=1, replica_groups=mesh['grp'=4,'sub'=8] {'sub'}, dimensions={0}, use_global_device_ids=true | all-gather | bytes 589824 | tf_op jit(solution)/shard_map/all_gather | solution.py:83
  186.5 25.4 %all_gather.33 = f32[1024,128]{1,0:T(8,128)S(1)} all-gather(f32[128,128]{1,0:T(8,128)S(1)} %get-tuple-element.215), channel_id=1, replica_groups=mesh['grp'=4,'sub'=8] {'sub'}, dimensions={0}, use_global_device_ids=true | all-gather | bytes 589824 | tf_op jit(solution)/shard_map/all_gather | solution.py:83
  212.5 25.6 %all_gather.34 = f32[1024,128]{1,0:T(8,128)S(1)} all-gather(f32[128,128]{1,0:T(8,128)S(1)} %get-tuple-element.217), channel_id=1, replica_groups=mesh['grp'=4,'sub'=8] {'sub'}, dimensions={0}, use_global_device_ids=true | all-gather | bytes 589824 | tf_op jit(solution)/shard_map/all_gather | solution.py:83
  240.8 30.2 %collective-permute-start.6 = (f32[64,128]{1,0:T(8,128)S(1)}, f32[64,128]{1,0:T(8,128)S(1)}, u32[]{:S(2)}, u32[]{:S(2)}) collective-permute-start(f32[64,128]{1,0:T(8,128)S(1)} %fusion.62), channel_id=1, source_target_pairs={{0,1},{1,2},{2,3},{3,4},{4,5},{5,6},{6,7},{7,8},{8,9},{9,10},{10,1... | collective-permute-start | bytes 98312 | tf_op jit(solution)/shard_map/ppermute | solution.py:18
  273.2 6.6 %collective-permute-done.7 = f32[64,128]{1,0:T(8,128)S(1)} collective-permute-done((f32[64,128]{1,0:T(8,128)S(1)}, f32[64,128]{1,0:T(8,128)S(1)}, u32[]{:S(2)}, u32[]{:S(2)}) %collective-permute-start.7) | collective-permute-done | bytes 32800 | tf_op jit(solution)/shard_map/ppermute | solution.py:18
  289.3 5.4 collective-permute-done.9
  318.9 5.4 collective-permute-done.13
  333.9 5.3 collective-permute-done.15
  348.6 5.4 collective-permute-done.17
  363.6 5.2 collective-permute-done.19
  373.0 24.9 %all_gather.35 = f32[1024,128]{1,0:T(8,128)S(1)} all-gather(f32[128,128]{1,0:T(8,128)S(1)} %get-tuple-element.219), channel_id=1, replica_groups=mesh['grp'=4,'sub'=8] {'sub'}, dimensions={0}, use_global_device_ids=true | all-gather | bytes 589824 | tf_op jit(solution)/shard_map/all_gather | solution.py:83
  398.5 25.4 %all_gather.36 = f32[1024,128]{1,0:T(8,128)S(1)} all-gather(f32[128,128]{1,0:T(8,128)S(1)} %get-tuple-element.221), channel_id=1, replica_groups=mesh['grp'=4,'sub'=8] {'sub'}, dimensions={0}, use_global_device_ids=true | all-gather | bytes 589824 | tf_op jit(solution)/shard_map/all_gather | solution.py:83
  424.6 26.1 %all_gather.37 = f32[1024,128]{1,0:T(8,128)S(1)} all-gather(f32[128,128]{1,0:T(8,128)S(1)} %get-tuple-element.223), channel_id=1, replica_groups=mesh['grp'=4,'sub'=8] {'sub'}, dimensions={0}, use_global_device_ids=true | all-gather | bytes 589824 | tf_op jit(solution)/shard_map/all_gather | solution.py:83
  451.3 25.9 %all_gather.38 = f32[1024,128]{1,0:T(8,128)S(1)} all-gather(f32[128,128]{1,0:T(8,128)S(1)} %get-tuple-element.225), channel_id=1, replica_groups=mesh['grp'=4,'sub'=8] {'sub'}, dimensions={0}, use_global_device_ids=true | all-gather | bytes 589824 | tf_op jit(solution)/shard_map/all_gather | solution.py:83
  477.8 25.3 %all_gather.39 = f32[1024,128]{1,0:T(8,128)S(1)} all-gather(f32[128,128]{1,0:T(8,128)S(1)} %get-tuple-element.227), channel_id=1, replica_groups=mesh['grp'=4,'sub'=8] {'sub'}, dimensions={0}, use_global_device_ids=true | all-gather | bytes 589824 | tf_op jit(solution)/shard_map/all_gather | solution.py:83
  505.8 31.2 %collective-permute-start.20 = (f32[64,128]{1,0:T(8,128)S(1)}, f32[64,128]{1,0:T(8,128)S(1)}, u32[]{:S(2)}, u32[]{:S(2)}) collective-permute-start(f32[64,128]{1,0:T(8,128)S(1)} %fusion.55), channel_id=1, source_target_pairs={{0,1},{1,2},{2,3},{3,4},{4,5},{5,6},{6,7},{7,8},{8,9},{9,10},{10,1... | collective-permute-start | bytes 98312 | tf_op jit(solution)/shard_map/ppermute | solution.py:18
  539.3 6.6 %collective-permute-done.21 = f32[64,128]{1,0:T(8,128)S(1)} collective-permute-done((f32[64,128]{1,0:T(8,128)S(1)}, f32[64,128]{1,0:T(8,128)S(1)}, u32[]{:S(2)}, u32[]{:S(2)}) %collective-permute-start.21) | collective-permute-done | bytes 32800 | tf_op jit(solution)/shard_map/ppermute | solution.py:18
  555.3 5.6 collective-permute-done.23
  586.5 5.4 collective-permute-done.27
  (176 shorter events, 165.1 us)
Async XLA Ops:
  4.9 65.7 %collective-permute-start.1 = (f32[64,128]{1,0:T(8,128)}, f32[64,128]{1,0:T(8,128)S(1)}, u32[]{:S(2)}, u32[]{:S(2)}) collective-permute-start(f32[64,128]{1,0:T(8,128)} %fusion.51), channel_id=1, source_target_pairs={{1,0},{2,1},{3,2},{4,3},{5,4},{6,5},{7,6},{8,7},{9,8},{10,9},{11,1... | collective-permute-start | bytes 98312 | tf_op jit(solution)/shard_map/ppermute | solution.py:18
  9.6 61.1 %collective-permute-start = (f32[64,128]{1,0:T(8,128)}, f32[64,128]{1,0:T(8,128)S(1)}, u32[]{:S(2)}, u32[]{:S(2)}) collective-permute-start(f32[64,128]{1,0:T(8,128)} %fusion.65), channel_id=1, source_target_pairs={{0,1},{1,2},{2,3},{3,4},{4,5},{5,6},{6,7},{7,8},{8,9},{9,10},{10,1... | collective-permute-start | bytes 98312 | tf_op jit(solution)/shard_map/ppermute | solution.py:18
  76.7 5.3 collective-permute-start.2
  78.7 8.8 %collective-permute-start.3 = (f32[64,128]{1,0:T(8,128)S(1)}, f32[64,128]{1,0:T(8,128)S(1)}, u32[]{:S(2)}, u32[]{:S(2)}) collective-permute-start(f32[64,128]{1,0:T(8,128)S(1)} %fusion.50), channel_id=1, source_target_pairs={{1,0},{2,1},{3,2},{4,3},{5,4},{6,5},{7,6},{8,7},{9,8},{10,9},{11,1... | collective-permute-start | bytes 98312 | tf_op jit(solution)/shard_map/ppermute | solution.py:18
  91.7 5.5 collective-permute-start.4
  93.6 8.8 %collective-permute-start.5 = (f32[64,128]{1,0:T(8,128)S(1)}, f32[64,128]{1,0:T(8,128)S(1)}, u32[]{:S(2)}, u32[]{:S(2)}) collective-permute-start(f32[64,128]{1,0:T(8,128)S(1)} %fusion.49), channel_id=1, source_target_pairs={{1,0},{2,1},{3,2},{4,3},{5,4},{6,5},{7,6},{8,7},{9,8},{10,9},{11,1... | collective-permute-start | bytes 98312 | tf_op jit(solution)/shard_map/ppermute | solution.py:18
  240.8 32.4 %collective-permute-start.6 = (f32[64,128]{1,0:T(8,128)S(1)}, f32[64,128]{1,0:T(8,128)S(1)}, u32[]{:S(2)}, u32[]{:S(2)}) collective-permute-start(f32[64,128]{1,0:T(8,128)S(1)} %fusion.62), channel_id=1, source_target_pairs={{0,1},{1,2},{2,3},{3,4},{4,5},{5,6},{6,7},{7,8},{8,9},{9,10},{10,1... | collective-permute-start | bytes 98312 | tf_op jit(solution)/shard_map/ppermute | solution.py:18
  271.0 8.8 %collective-permute-start.7 = (f32[64,128]{1,0:T(8,128)S(1)}, f32[64,128]{1,0:T(8,128)S(1)}, u32[]{:S(2)}, u32[]{:S(2)}) collective-permute-start(f32[64,128]{1,0:T(8,128)S(1)} %fusion.48), channel_id=1, source_target_pairs={{1,0},{2,1},{3,2},{4,3},{5,4},{6,5},{7,6},{8,7},{9,8},{10,9},{11,1... | collective-permute-start | bytes 98312 | tf_op jit(solution)/shard_map/ppermute | solution.py:18
  284.0 5.3 collective-permute-start.8
  285.9 8.8 %collective-permute-start.9 = (f32[64,128]{1,0:T(8,128)S(1)}, f32[64,128]{1,0:T(8,128)S(1)}, u32[]{:S(2)}, u32[]{:S(2)}) collective-permute-start(f32[64,128]{1,0:T(8,128)S(1)} %fusion.47), channel_id=1, source_target_pairs={{1,0},{2,1},{3,2},{4,3},{5,4},{6,5},{7,6},{8,7},{9,8},{10,9},{11,1... | collective-permute-start | bytes 98312 | tf_op jit(solution)/shard_map/ppermute | solution.py:18
  298.8 5.8 collective-permute-start.10
  300.7 8.8 %collective-permute-start.11 = (f32[64,128]{1,0:T(8,128)S(1)}, f32[64,128]{1,0:T(8,128)S(1)}, u32[]{:S(2)}, u32[]{:S(2)}) collective-permute-start(f32[64,128]{1,0:T(8,128)S(1)} %fusion.46), channel_id=1, source_target_pairs={{1,0},{2,1},{3,2},{4,3},{5,4},{6,5},{7,6},{8,7},{9,8},{10,9},{11,1... | collective-permute-start | bytes 98312 | tf_op jit(solution)/shard_map/ppermute | solution.py:18
  315.5 8.8 %collective-permute-start.13 = (f32[64,128]{1,0:T(8,128)S(1)}, f32[64,128]{1,0:T(8,128)S(1)}, u32[]{:S(2)}, u32[]{:S(2)}) collective-permute-start(f32[64,128]{1,0:T(8,128)S(1)} %fusion.45), channel_id=1, source_target_pairs={{1,0},{2,1},{3,2},{4,3},{5,4},{6,5},{7,6},{8,7},{9,8},{10,9},{11,1... | collective-permute-start | bytes 98312 | tf_op jit(solution)/shard_map/ppermute | solution.py:18
  328.4 5.5 collective-permute-start.14
  330.3 8.8 %collective-permute-start.15 = (f32[64,128]{1,0:T(8,128)S(1)}, f32[64,128]{1,0:T(8,128)S(1)}, u32[]{:S(2)}, u32[]{:S(2)}) collective-permute-start(f32[64,128]{1,0:T(8,128)S(1)} %fusion.44), channel_id=1, source_target_pairs={{1,0},{2,1},{3,2},{4,3},{5,4},{6,5},{7,6},{8,7},{9,8},{10,9},{11,1... | collective-permute-start | bytes 98312 | tf_op jit(solution)/shard_map/ppermute | solution.py:18
  345.2 8.8 %collective-permute-start.17 = (f32[64,128]{1,0:T(8,128)S(1)}, f32[64,128]{1,0:T(8,128)S(1)}, u32[]{:S(2)}, u32[]{:S(2)}) collective-permute-start(f32[64,128]{1,0:T(8,128)S(1)} %fusion.43), channel_id=1, source_target_pairs={{1,0},{2,1},{3,2},{4,3},{5,4},{6,5},{7,6},{8,7},{9,8},{10,9},{11,1... | collective-permute-start | bytes 98312 | tf_op jit(solution)/shard_map/ppermute | solution.py:18
  358.1 5.5 collective-permute-start.18
  360.0 8.8 %collective-permute-start.19 = (f32[64,128]{1,0:T(8,128)S(1)}, f32[64,128]{1,0:T(8,128)S(1)}, u32[]{:S(2)}, u32[]{:S(2)}) collective-permute-start(f32[64,128]{1,0:T(8,128)S(1)} %fusion.42), channel_id=1, source_target_pairs={{1,0},{2,1},{3,2},{4,3},{5,4},{6,5},{7,6},{8,7},{9,8},{10,9},{11,1... | collective-permute-start | bytes 98312 | tf_op jit(solution)/shard_map/ppermute | solution.py:18
  505.8 33.4 %collective-permute-start.20 = (f32[64,128]{1,0:T(8,128)S(1)}, f32[64,128]{1,0:T(8,128)S(1)}, u32[]{:S(2)}, u32[]{:S(2)}) collective-permute-start(f32[64,128]{1,0:T(8,128)S(1)} %fusion.55), channel_id=1, source_target_pairs={{0,1},{1,2},{2,3},{3,4},{4,5},{5,6},{6,7},{7,8},{8,9},{9,10},{10,1... | collective-permute-start | bytes 98312 | tf_op jit(solution)/shard_map/ppermute | solution.py:18
  537.1 8.8 %collective-permute-start.21 = (f32[64,128]{1,0:T(8,128)S(1)}, f32[64,128]{1,0:T(8,128)S(1)}, u32[]{:S(2)}, u32[]{:S(2)}) collective-permute-start(f32[64,128]{1,0:T(8,128)S(1)} %fusion.41), channel_id=1, source_target_pairs={{1,0},{2,1},{3,2},{4,3},{5,4},{6,5},{7,6},{8,7},{9,8},{10,9},{11,1... | collective-permute-start | bytes 98312 | tf_op jit(solution)/shard_map/ppermute | solution.py:18
  551.9 8.9 %collective-permute-start.23 = (f32[64,128]{1,0:T(8,128)S(1)}, f32[64,128]{1,0:T(8,128)S(1)}, u32[]{:S(2)}, u32[]{:S(2)}) collective-permute-start(f32[64,128]{1,0:T(8,128)S(1)} %fusion.40), channel_id=1, source_target_pairs={{1,0},{2,1},{3,2},{4,3},{5,4},{6,5},{7,6},{8,7},{9,8},{10,9},{11,1... | collective-permute-start | bytes 98312 | tf_op jit(solution)/shard_map/ppermute | solution.py:18
  564.9 5.6 collective-permute-start.24
  566.9 8.8 %collective-permute-start.25 = (f32[64,128]{1,0:T(8,128)S(1)}, f32[64,128]{1,0:T(8,128)S(1)}, u32[]{:S(2)}, u32[]{:S(2)}) collective-permute-start(f32[64,128]{1,0:T(8,128)S(1)} %fusion.39), channel_id=1, source_target_pairs={{1,0},{2,1},{3,2},{4,3},{5,4},{6,5},{7,6},{8,7},{9,8},{10,9},{11,1... | collective-permute-start | bytes 98312 | tf_op jit(solution)/shard_map/ppermute | solution.py:18
  583.1 8.8 %collective-permute-start.27 = (f32[64,128]{1,0:T(8,128)S(1)}, f32[64,128]{1,0:T(8,128)S(1)}, u32[]{:S(2)}, u32[]{:S(2)}) collective-permute-start(f32[64,128]{1,0:T(8,128)S(1)} %fusion.38), channel_id=1, source_target_pairs={{1,0},{2,1},{3,2},{4,3},{5,4},{6,5},{7,6},{8,7},{9,8},{10,9},{11,1... | collective-permute-start | bytes 98312 | tf_op jit(solution)/shard_map/ppermute | solution.py:18
  (12 other events, 89.7 us)
where the time goes:
time: 600 us; the launch traced here: 596 us
  blocking collectives  256 us (43%)
  starting transfers between devices  135 us (22%)
  waiting for transfers between devices  72 us (12%)
  matrix products  64.9 us (11%)
  other arithmetic  61.3 us (10%)
    all_gather x10, blocking collectives, apply_coarse(): whole = lax.all_gather(vector, 'sub', axis=0, tiled=True)  256 us
    ppermute x28, starting transfers between devices, from_behind(): return lax.ppermute(shard, axis, pairs)  135 us
    ppermute x28, waiting for transfers between devices, from_behind(): return lax.ppermute(shard, axis, pairs)  72 us
    add x1, other arithmetic, band_tiles(): tiles + jnp.where(local[entry][:, None] == places, fine_values[entry][:,...  47.7 us
    dot_general x14, matrix products, fine_apply(): jnp.einsum('brc,bcn->brn', low_tiles, pieces[:-1], precision=highest)  17.3 us
    dot_general x14, matrix products, fine_apply(): jnp.einsum('brc,bcn->brn', high_tiles, pieces[1:], precision=highest)  16.8 us
  transfers between devices with their start and end apart: 28, of which 13 were waited for; matrix products, arithmetic and copies ran while one was open for 9% of the time, Pallas kernels for 0%

commit v1 on v0

--- a/solution.py
+++ b/solution.py
@@ -80,7 +80,14 @@
     coarse_inverse = 1.0 / jnp.diagonal(block)[:, None]
 
     def apply_coarse(vector):
-        whole = lax.all_gather(vector, "sub", axis=0, tiled=True)
+        peers_2 = lax.axis_size("sub")
+        forward = [(i_2, (i_2 + 1) % peers_2) for i_2 in range(peers_2)]
+        parts = [vector]
+        for far in range(1, peers_2):
+            parts = [lax.ppermute(parts[0], "sub", forward), *parts]
+        out = jnp.concatenate(parts, axis=0)
+        offset = (lax.axis_index("sub") + 1) * parts[-1].shape[0]
+        whole = jnp.roll(out, offset, axis=0)
         return jnp.dot(own_rows, whole, precision=highest)
 
     dinv = 1.0 / fine_values[0][:, None]

time: 600 us -> 782 us (1.30)
  starting transfers between devices: 135 us -> 469 us
  blocking collectives: 256 us -> 0 us
  waiting for transfers between devices: 72 us -> 171 us
    ppermute x0 -> x70, starting transfers between devices: none -> 305 us  [apply_coarse(): parts = [lax.ppermute(parts[0], 'sub', forward), *parts]]
    all_gather x10 -> x0, blocking collectives: 256 us -> none  [apply_coarse(): whole = lax.all_gather(vector, 'sub', axis=0, tiled=True)]
    ppermute x0 -> x70, waiting for transfers between devices: none -> 99.8 us  [apply_coarse(): parts = [lax.ppermute(parts[0], 'sub', forward), *parts]]
    ppermute x28, starting transfers between devices: 135 us -> 164 us  [from_behind(): return lax.ppermute(shard, axis, pairs)]
  transfers between devices with their start and end apart: 28 -> 98, of which waited for: 13 -> 83; matrix products, arithmetic and copies ran while one was open for 9% -> 7% of each run, Pallas kernels for 0% -> 0%
where the time goes in v1:
time: 782 us; the launch traced here: 778 us
  starting transfers between devices  469 us (60%)
  waiting for transfers between devices  171 us (22%)
  matrix products  67 us (9%)
  other arithmetic  61.8 us (8%)
    ppermute x70, starting transfers between devices, apply_coarse(): parts = [lax.ppermute(parts[0], 'sub', forward), *parts]  305 us
    ppermute x28, starting transfers between devices, from_behind(): return lax.ppermute(shard, axis, pairs)  164 us
    ppermute x70, waiting for transfers between devices, apply_coarse(): parts = [lax.ppermute(parts[0], 'sub', forward), *parts]  99.8 us
    ppermute x28, waiting for transfers between devices, from_behind(): return lax.ppermute(shard, axis, pairs)  71.1 us
    add x1, other arithmetic, band_tiles(): tiles + jnp.where(local[entry][:, None] == places, fine_values[entry][:,...  46.7 us
    dot_general x14, matrix products, fine_apply(): jnp.einsum('brc,bcn->brn', low_tiles, pieces[:-1], precision=highest)  17.3 us
    dot_general x14, matrix products, fine_apply(): jnp.einsum('brc,bcn->brn', high_tiles, pieces[1:], precision=highest)  16.7 us
  transfers between devices with their start and end apart: 98, of which 83 were waited for; matrix products, arithmetic and copies ran while one was open for 7% of the time, Pallas kernels for 0%

profile of v1, /device:TPU:29, one launch (start us, length us, event | category | flops | bytes accessed | tf_op | source)
XLA Modules:
  0.0 778.3 jit_solution(14343688523462818853)
XLA Ops:
  9.5 7.1 collective-permute-start
  21.5 46.7 %select_add_fusion = f32[16,128,256]{2,1,0:T(8,128)S(1)} fusion(f32[16,128]{1,0:T(8,128)S(1)} %bitcast.476, s32[16,128]{1,0:T(8,128)} %bitcast.598, f32[16,128]{1,0:T(8,128)S(1)} %bitcast.477, s32[16,128]{1,0:T(8,128)} %bitcast.599, f32[16,128]{1,0:T(8,128)S(1)} %bitcast.455, s32[16,128]{1,0:T(8,128)} %bitcast.600, f32[16,128]{1,0:T(8,128)S(1)} %bitcast.456, ...), kind=kLoop, calls=%fused_computation.1 | loop fusion | flops 126877696 | bytes 3424256 | tf_op jit(solution)/shard_map/add | solution.py:29
  97.2 5.0 collective-permute-done.5
  119.9 5.0 collective-permute-start.9
  156.9 4.9 collective-permute-start.15
  199.5 4.7 collective-permute-start.22
  229.9 4.7 collective-permute-start.27
  307.3 5.0 collective-permute-start.40
  316.7 45.2 %collective-permute-start.41 = (f32[64,128]{1,0:T(8,128)S(1)}, f32[64,128]{1,0:T(8,128)S(1)}, u32[]{:S(2)}, u32[]{:S(2)}) collective-permute-start(f32[64,128]{1,0:T(8,128)S(1)} %fusion.82), channel_id=1, source_target_pairs={{0,1},{1,2},{2,3},{3,4},{4,5},{5,6},{6,7},{7,8},{8,9},{9,10},{10,1... | collective-permute-start | bytes 98312 | tf_op jit(solution)/shard_map/ppermute | solution.py:18
  363.9 6.9 collective-permute-done.42
  380.1 5.4 collective-permute-done.44
  395.1 5.3 collective-permute-done.46
  409.9 5.4 collective-permute-done.48
  425.1 5.0 collective-permute-done.50
  439.5 5.4 collective-permute-done.52
  454.5 5.3 collective-permute-done.54
  494.9 4.9 collective-permute-start.61
  646.2 4.7 collective-permute-start.86
  663.8 4.7 collective-permute-start.89
  672.9 46.3 %collective-permute-start.90 = (f32[64,128]{1,0:T(8,128)S(1)}, f32[64,128]{1,0:T(8,128)S(1)}, u32[]{:S(2)}, u32[]{:S(2)}) collective-permute-start(f32[64,128]{1,0:T(8,128)S(1)} %fusion.75), channel_id=1, source_target_pairs={{0,1},{1,2},{2,3},{3,4},{4,5},{5,6},{6,7},{7,8},{8,9},{9,10},{10,1... | collective-permute-start | bytes 98312 | tf_op jit(solution)/shard_map/ppermute | solution.py:18
  721.2 6.9 collective-permute-done.91
  737.4 5.4 collective-permute-done.93
  752.5 5.2 collective-permute-done.95
  768.8 5.4 collective-permute-done.97
  (402 shorter events, 524.8 us)
Async XLA Ops:
  4.9 63.4 %collective-permute-start.1 = (f32[64,128]{1,0:T(8,128)}, f32[64,128]{1,0:T(8,128)S(1)}, u32[]{:S(2)}, u32[]{:S(2)}) collective-permute-start(f32[64,128]{1,0:T(8,128)} %fusion.71), channel_id=1, source_target_pairs={{1,0},{2,1},{3,2},{4,3},{5,4},{6,5},{7,6},{8,7},{9,8},{10,9},{11,1... | collective-permute-start | bytes 98312 | tf_op jit(solution)/shard_map/ppermute | solution.py:18
  9.5 58.8 %collective-permute-start = (f32[64,128]{1,0:T(8,128)}, f32[64,128]{1,0:T(8,128)S(1)}, u32[]{:S(2)}, u32[]{:S(2)}) collective-permute-start(f32[64,128]{1,0:T(8,128)} %fusion.85), channel_id=1, source_target_pairs={{0,1},{1,2},{2,3},{3,4},{4,5},{5,6},{6,7},{7,8},{8,9},{9,10},{10,1... | collective-permute-start | bytes 98312 | tf_op jit(solution)/shard_map/ppermute | solution.py:18
  74.8 6.6 collective-permute-start.2
  76.8 8.8 %collective-permute-start.3 = (f32[64,128]{1,0:T(8,128)S(1)}, f32[64,128]{1,0:T(8,128)S(1)}, u32[]{:S(2)}, u32[]{:S(2)}) collective-permute-start(f32[64,128]{1,0:T(8,128)S(1)} %fusion.70), channel_id=1, source_target_pairs={{1,0},{2,1},{3,2},{4,3},{5,4},{6,5},{7,6},{8,7},{9,8},{10,9},{11,1... | collective-permute-start | bytes 98312 | tf_op jit(solution)/shard_map/ppermute | solution.py:18
  93.4 8.8 %collective-permute-start.5 = (f32[64,128]{1,0:T(8,128)S(1)}, f32[64,128]{1,0:T(8,128)S(1)}, u32[]{:S(2)}, u32[]{:S(2)}) collective-permute-start(f32[64,128]{1,0:T(8,128)S(1)} %fusion.69), channel_id=1, source_target_pairs={{1,0},{2,1},{3,2},{4,3},{5,4},{6,5},{7,6},{8,7},{9,8},{10,9},{11,1... | collective-permute-start | bytes 98312 | tf_op jit(solution)/shard_map/ppermute | solution.py:18
  119.9 6.4 collective-permute-start.9
  150.6 6.3 collective-permute-start.14
  193.3 6.3 collective-permute-start.21
  229.9 6.3 collective-permute-start.27
  307.3 6.3 collective-permute-start.40
  316.7 47.1 %collective-permute-start.41 = (f32[64,128]{1,0:T(8,128)S(1)}, f32[64,128]{1,0:T(8,128)S(1)}, u32[]{:S(2)}, u32[]{:S(2)}) collective-permute-start(f32[64,128]{1,0:T(8,128)S(1)} %fusion.82), channel_id=1, source_target_pairs={{0,1},{1,2},{2,3},{3,4},{4,5},{5,6},{6,7},{7,8},{8,9},{9,10},{10,1... | collective-permute-start | bytes 98312 | tf_op jit(solution)/shard_map/ppermute | solution.py:18
  361.9 8.8 %collective-permute-start.42 = (f32[64,128]{1,0:T(8,128)S(1)}, f32[64,128]{1,0:T(8,128)S(1)}, u32[]{:S(2)}, u32[]{:S(2)}) collective-permute-start(f32[64,128]{1,0:T(8,128)S(1)} %fusion.68), channel_id=1, source_target_pairs={{1,0},{2,1},{3,2},{4,3},{5,4},{6,5},{7,6},{8,7},{9,8},{10,9},{11,1... | collective-permute-start | bytes 98312 | tf_op jit(solution)/shard_map/ppermute | solution.py:18
  376.7 8.8 %collective-permute-start.44 = (f32[64,128]{1,0:T(8,128)S(1)}, f32[64,128]{1,0:T(8,128)S(1)}, u32[]{:S(2)}, u32[]{:S(2)}) collective-permute-start(f32[64,128]{1,0:T(8,128)S(1)} %fusion.67), channel_id=1, source_target_pairs={{1,0},{2,1},{3,2},{4,3},{5,4},{6,5},{7,6},{8,7},{9,8},{10,9},{11,1... | collective-permute-start | bytes 98312 | tf_op jit(solution)/shard_map/ppermute | solution.py:18
  391.5 8.9 %collective-permute-start.46 = (f32[64,128]{1,0:T(8,128)S(1)}, f32[64,128]{1,0:T(8,128)S(1)}, u32[]{:S(2)}, u32[]{:S(2)}) collective-permute-start(f32[64,128]{1,0:T(8,128)S(1)} %fusion.66), channel_id=1, source_target_pairs={{1,0},{2,1},{3,2},{4,3},{5,4},{6,5},{7,6},{8,7},{9,8},{10,9},{11,1... | collective-permute-start | bytes 98312 | tf_op jit(solution)/shard_map/ppermute | solution.py:18
  406.5 8.8 %collective-permute-start.48 = (f32[64,128]{1,0:T(8,128)S(1)}, f32[64,128]{1,0:T(8,128)S(1)}, u32[]{:S(2)}, u32[]{:S(2)}) collective-permute-start(f32[64,128]{1,0:T(8,128)S(1)} %fusion.65), channel_id=1, source_target_pairs={{1,0},{2,1},{3,2},{4,3},{5,4},{6,5},{7,6},{8,7},{9,8},{10,9},{11,1... | collective-permute-start | bytes 98312 | tf_op jit(solution)/shard_map/ppermute | solution.py:18
  421.3 8.8 %collective-permute-start.50 = (f32[64,128]{1,0:T(8,128)S(1)}, f32[64,128]{1,0:T(8,128)S(1)}, u32[]{:S(2)}, u32[]{:S(2)}) collective-permute-start(f32[64,128]{1,0:T(8,128)S(1)} %fusion.64), channel_id=1, source_target_pairs={{1,0},{2,1},{3,2},{4,3},{5,4},{6,5},{7,6},{8,7},{9,8},{10,9},{11,1... | collective-permute-start | bytes 98312 | tf_op jit(solution)/shard_map/ppermute | solution.py:18
  436.1 8.8 %collective-permute-start.52 = (f32[64,128]{1,0:T(8,128)S(1)}, f32[64,128]{1,0:T(8,128)S(1)}, u32[]{:S(2)}, u32[]{:S(2)}) collective-permute-start(f32[64,128]{1,0:T(8,128)S(1)} %fusion.63), channel_id=1, source_target_pairs={{1,0},{2,1},{3,2},{4,3},{5,4},{6,5},{7,6},{8,7},{9,8},{10,9},{11,1... | collective-permute-start | bytes 98312 | tf_op jit(solution)/shard_map/ppermute | solution.py:18
  451.0 8.8 %collective-permute-start.54 = (f32[64,128]{1,0:T(8,128)S(1)}, f32[64,128]{1,0:T(8,128)S(1)}, u32[]{:S(2)}, u32[]{:S(2)}) collective-permute-start(f32[64,128]{1,0:T(8,128)S(1)} %fusion.62), channel_id=1, source_target_pairs={{1,0},{2,1},{3,2},{4,3},{5,4},{6,5},{7,6},{8,7},{9,8},{10,9},{11,1... | collective-permute-start | bytes 98312 | tf_op jit(solution)/shard_map/ppermute | solution.py:18
  488.5 6.3 collective-permute-start.60
  672.9 48.2 %collective-permute-start.90 = (f32[64,128]{1,0:T(8,128)S(1)}, f32[64,128]{1,0:T(8,128)S(1)}, u32[]{:S(2)}, u32[]{:S(2)}) collective-permute-start(f32[64,128]{1,0:T(8,128)S(1)} %fusion.75), channel_id=1, source_target_pairs={{0,1},{1,2},{2,3},{3,4},{4,5},{5,6},{6,7},{7,8},{8,9},{9,10},{10,1... | collective-permute-start | bytes 98312 | tf_op jit(solution)/shard_map/ppermute | solution.py:18
  719.2 8.8 %collective-permute-start.91 = (f32[64,128]{1,0:T(8,128)S(1)}, f32[64,128]{1,0:T(8,128)S(1)}, u32[]{:S(2)}, u32[]{:S(2)}) collective-permute-start(f32[64,128]{1,0:T(8,128)S(1)} %fusion.61), channel_id=1, source_target_pairs={{1,0},{2,1},{3,2},{4,3},{5,4},{6,5},{7,6},{8,7},{9,8},{10,9},{11,1... | collective-permute-start | bytes 98312 | tf_op jit(solution)/shard_map/ppermute | solution.py:18
  734.0 8.8 %collective-permute-start.93 = (f32[64,128]{1,0:T(8,128)S(1)}, f32[64,128]{1,0:T(8,128)S(1)}, u32[]{:S(2)}, u32[]{:S(2)}) collective-permute-start(f32[64,128]{1,0:T(8,128)S(1)} %fusion.60), channel_id=1, source_target_pairs={{1,0},{2,1},{3,2},{4,3},{5,4},{6,5},{7,6},{8,7},{9,8},{10,9},{11,1... | collective-permute-start | bytes 98312 | tf_op jit(solution)/shard_map/ppermute | solution.py:18
  748.8 8.8 %collective-permute-start.95 = (f32[64,128]{1,0:T(8,128)S(1)}, f32[64,128]{1,0:T(8,128)S(1)}, u32[]{:S(2)}, u32[]{:S(2)}) collective-permute-start(f32[64,128]{1,0:T(8,128)S(1)} %fusion.59), channel_id=1, source_target_pairs={{1,0},{2,1},{3,2},{4,3},{5,4},{6,5},{7,6},{8,7},{9,8},{10,9},{11,1... | collective-permute-start | bytes 98312 | tf_op jit(solution)/shard_map/ppermute | solution.py:18
  765.4 8.8 %collective-permute-start.97 = (f32[64,128]{1,0:T(8,128)S(1)}, f32[64,128]{1,0:T(8,128)S(1)}, u32[]{:S(2)}, u32[]{:S(2)}) collective-permute-start(f32[64,128]{1,0:T(8,128)S(1)} %fusion.58), channel_id=1, source_target_pairs={{1,0},{2,1},{3,2},{4,3},{5,4},{6,5},{7,6},{8,7},{9,8},{10,9},{11,1... | collective-permute-start | bytes 98312 | tf_op jit(solution)/shard_map/ppermute | solution.py:18
  (90 other events, 560.6 us)
